TPU v7x, 512 devices: a whole 4x8x8 slice. The times are simulated.
512 devices in a mesh: occ: 16 (over y, core), vir: 32 (over x, z).
Axes of the slice: x: 4, y: 8, z: 8, core: 2. Of those that a mesh axis runs over, the one named last changes fastest.
Arguments:
- amplitudes: float32 [2048, 12288], P('occ', 'vir'), may hold values from -6 to 6
- integrals: float32 [12288, 4096], P('vir', 'occ'), may hold values from -0.109375 to 0.109375
- pair_mask: int32 [32, 192], P('occ', 'vir'), may hold values 0 or 1
- tile_mask: int32 [192, 64], P('vir', 'occ'), may hold values 0 or 1
Outputs:
- residual: float32 [2048, 4096], P('occ', 'vir')
Inputs may be any that keep to these rules, and one draw needn't show every extreme that they name: `pair_mask`: 0 marks a tile that is absent and contributes nothing. `tile_mask`: 0 marks a tile that is absent and contributes nothing.
All inputs are finite; a program needn't handle non-finite values. No bound on the sum of `pair_mask` or of `tile_mask` on one device may be relied on, other than what follows from the above.
Results may differ from a plain program's by a relative error of at most 0.00007.
Values sent between devices are 32-bit elements; how exact they have to be, the bound alone decides.
No kernel may reach another device: no remote copies, remote signals or barrier semaphores. Data moves between devices by JAX's collectives and lax.ppermute only.
A program may use at most 64 MiB of HBM per device.

v0:
```python
import jax
import jax.numpy as jnp
from jax import lax
from jax.sharding import PartitionSpec as P


def expand(mask, width):
    grown = jnp.repeat(mask.astype(jnp.float32), width, axis=0)
    return jnp.repeat(grown, width, axis=1)


def body(amplitudes, integrals, pair_mask, tile_mask):
    tile_width = amplitudes.shape[1] // pair_mask.shape[1]
    masked_t = amplitudes * expand(pair_mask, tile_width)
    masked_v = integrals * expand(tile_mask, tile_width)
    partial_sum = jnp.dot(
        masked_t,
        lax.all_gather(masked_v, "occ", axis=1, tiled=True),
        precision=lax.Precision.HIGHEST,
        preferred_element_type=jnp.float32,
    )
    return lax.psum_scatter(partial_sum, "vir", scatter_dimension=1, tiled=True)


def solution(mesh):
    in_specs = (P("occ", "vir"), P("vir", "occ"), P("occ", "vir"), P("vir", "occ"))
    out_specs = P("occ", "vir")
    return jax.shard_map(body, mesh=mesh, in_specs=in_specs, out_specs=out_specs, check_vma=False)
```

profile of v0, /device:TPU:8, one launch (start us, length us, event | category | flops | bytes accessed | tf_op | source)
XLA Modules:
  0.0 302.7 jit_solution(3729471157549326904)
XLA Ops:
  6.5 0.0 all-gather.2.cloned.1.call-start
  6.5 0.7 convert_element_type.7
  7.2 0.1 broadcast_in_dim.14
  7.3 0.1 reshape.14
  7.4 1.2 copy.11
  8.5 0.8 bitcast_multiply_fusion
  9.3 0.0 all-gather.2.cloned.1.call-update
  9.3 0.0 reduce-scatter.2.cloned.1.call-start
  9.4 0.7 convert_element_type.6
  10.1 0.1 copy.9
  10.2 0.1 broadcast_in_dim.12
  10.2 0.1 reshape.12
  10.3 1.1 copy.10
  11.4 51.0 %all-gather.2.cloned.1.call-done = f32[384,4096]{0,1:T(8,128)} async-done(((f32[384,256]{0,1:T(8,128)}), f32[384,4096]{0,1:T(8,128)}) %all-gather.2.cloned.1.call-update) | async-done | bytes 6291472 | tf_op jit(solution)/shard_map/all_gather | solution.py:18
  62.4 10.7 %fusion = f32[128,4096]{1,0:T(8,128)} fusion(f32[128,384]{0,1:T(8,128)S(1)} %bitcast_multiply_fusion.1, f32[384,4096]{0,1:T(8,128)} %all-gather.2.cloned.1.call-done), kind=kOutput, calls=%fused_computation.2 | convolution fusion | flops 2415919104 | bytes 8585216 | tf_op jit(solution)/shard_map/dot_general | solution.py:16
  73.0 0.0 reduce-scatter.2.cloned.1.call-update
  73.1 222.8 %reduce-scatter.2.cloned.1.call-done = f32[128,128]{1,0:T(8,128)} async-done(((f32[128,4096]{1,0:T(8,128)}), f32[128,128]{1,0:T(8,128)}) %reduce-scatter.2.cloned.1.call-update) | async-done | bytes 65552 | tf_op jit(solution)/shard_map/reduce_scatter | solution.py:22
  (1 shorter events, 0.0 us)
Async XLA Ops:
  6.5 55.9 %all-gather.2.cloned.1.call-start = ((), (), s32[]{:S(2)}) async-start(), calls=%async_computation.1 | async-start | bytes 6684672 | tf_op jit(solution)/shard_map/all_gather | solution.py:18
  9.3 286.5 %reduce-scatter.2.cloned.1.call-start = ((), (), s32[]{:S(2)}) async-start(), calls=%async_computation.2 | async-start | bytes 2162688 | tf_op jit(solution)/shard_map/reduce_scatter | solution.py:22
Sparse Core Ops, SparseCore 0:
  9.5 52.8 all-gather.1
  73.2 222.6 reduce-scatter.1
where the time goes:
time: 303 us
  waiting for transfers between devices  274 us (90%)
  between operations  13.4 us (4%)
  matrix products  10.7 us (4%)
    reduce_scatter x1, waiting for transfers between devices, body(): return lax.psum_scatter(partial_sum, 'vir', scatter_dimension=1, tiled=True)  223 us
    all_gather x1, waiting for transfers between devices, body(): lax.all_gather(masked_v, 'occ', axis=1, tiled=True)  51 us
    dot_general x1, matrix products, body(): jnp.dot(masked_t, lax.all_gather(masked_v, 'occ', axis=1, tiled=True), pr...  10.7 us
  transfers between devices with their start and end apart: 2, of which 2 were waited for; matrix products, arithmetic and copies ran while one was open for 1% of the time, Pallas kernels for 0%

commit v1 on v0

--- a/solution.py
+++ b/solution.py
@@ -15,7 +15,9 @@
     masked_v = integrals * expand(tile_mask, tile_width)
     partial_sum = jnp.dot(
         masked_t,
-        lax.all_gather(masked_v, "occ", axis=1, tiled=True),
+        jnp.concatenate(
+            lax.all_to_all(jnp.stack([masked_v] * lax.axis_size("occ")), "occ", 0, 0), axis=1
+        ),
         precision=lax.Precision.HIGHEST,
         preferred_element_type=jnp.float32,
     )

time: 303 us -> 402 us (1.33)
  waiting for transfers between devices: 274 us -> 362 us
  starting transfers between devices: 0.04 us -> 10.4 us
    all_to_all x0 -> x1, waiting for transfers between devices: none -> 137 us  [body(): lax.all_to_all(jnp.stack([masked_v] * lax.axis_size('occ')), 'occ', 0, 0)]
    all_gather x1 -> x0, waiting for transfers between devices: 51 us -> none  [body(): lax.all_gather(masked_v, 'occ', axis=1, tiled=True)]
    all_to_all x0 -> x1, starting transfers between devices: none -> 10.3 us  [body(): lax.all_to_all(jnp.stack([masked_v] * lax.axis_size('occ')), 'occ', 0, 0)]
  transfers between devices with their start and end apart: 2 -> 2, of which waited for: 2 -> 2; matrix products, arithmetic and copies ran while one was open for 1% -> 0% of each run, Pallas kernels for 0% -> 0%
where the time goes in v1:
time: 402 us
  waiting for transfers between devices  362 us (90%)
  between operations  13.5 us (3%)
  matrix products  10.6 us (3%)
  starting transfers between devices  10.4 us (3%)
  local copies, waits for them, and re-layouts  4.95 us (1%)
    reduce_scatter x1, waiting for transfers between devices, body(): return lax.psum_scatter(partial_sum, 'vir', scatter_dimension=1, tiled=True)  225 us
    all_to_all x1, waiting for transfers between devices, body(): lax.all_to_all(jnp.stack([masked_v] * lax.axis_size('occ')), 'occ', 0, 0)  137 us
    dot_general x1, matrix products, body(): jnp.dot(masked_t, jnp.concatenate(lax.all_to_all(jnp.stack([masked_v] * l...  10.6 us
    all_to_all x1, starting transfers between devices, body(): lax.all_to_all(jnp.stack([masked_v] * lax.axis_size('occ')), 'occ', 0, 0)  10.3 us
  transfers between devices with their start and end apart: 2, of which 2 were waited for; matrix products, arithmetic and copies ran while one was open for 0% of the time, Pallas kernels for 0%

profile of v1, /device:TPU:8, one launch (start us, length us, event | category | flops | bytes accessed | tf_op | source)
XLA Modules:
  0.0 401.9 jit_solution(9843134684687615133)
XLA Ops:
  6.5 1.2 copy.11
  7.7 0.7 convert_element_type.7
  8.4 0.1 broadcast_in_dim.14
  8.5 0.1 reshape.22
  8.6 3.3 stack.2
  11.8 0.0 copy-start
  11.8 0.0 copy-start.1
  11.8 10.3 %all-to-all-start = ((f32[16,384,256]{1,2,0:T(8,128)}), f32[16,384,256]{1,2,0:T(8,128)}, u32[]{:S(2)}, u32[]{:S(2)}) async-start(f32[16,384,256]{1,2,0:T(8,128)} %stack.2), calls=%async_computation | async-start | bytes 12582912 | tf_op jit(solution)/shard_map/all_to_all | solution.py:19
  22.2 0.0 reduce-scatter.2.cloned.1.call-start
  22.2 0.0 copy-done
  22.2 0.1 copy.10
  22.4 0.0 copy-done.1
  22.4 0.1 copy.9
  22.5 0.1 broadcast_in_dim.12
  22.5 0.1 reshape.20
  22.7 137.0 %all-to-all-done = f32[16,384,256]{1,2,0:T(8,128)} async-done(((f32[16,384,256]{1,2,0:T(8,128)}), f32[16,384,256]{1,2,0:T(8,128)}, u32[]{:S(2)}, u32[]{:S(2)}) %all-to-all-start) | async-done | bytes 6291488 | tf_op jit(solution)/shard_map/all_to_all | solution.py:19
  159.6 10.6 %fusion = f32[128,4096]{1,0:T(8,128)} fusion(f32[128,384]{0,1:T(8,128)S(1)} %bitcast_multiply_fusion.1, f32[384,4096]{0,1:T(8,128)} %bitcast.3), kind=kOutput, calls=%fused_computation.2 | convolution fusion | flops 2415919104 | bytes 8585216 | tf_op jit(solution)/shard_map/dot_general | solution.py:16
  170.3 0.0 reduce-scatter.2.cloned.1.call-update
  170.3 224.7 %reduce-scatter.2.cloned.1.call-done = f32[128,128]{1,0:T(8,128)} async-done(((f32[128,4096]{1,0:T(8,128)}), f32[128,128]{1,0:T(8,128)}) %reduce-scatter.2.cloned.1.call-update) | async-done | bytes 65552 | tf_op jit(solution)/shard_map/reduce_scatter | solution.py:24
  (3 shorter events, 0.1 us)
Async XLA Ops:
  11.8 10.4 %copy-start = (f32[128,384]{1,0:T(8,128)S(1)}, f32[128,384]{1,0:T(8,128)}, u32[]{:S(2)}) copy-start(f32[128,384]{1,0:T(8,128)} %param.4) | copy-start | bytes 589828
  11.8 10.5 %copy-start.1 = (s32[2,6]{1,0:T(2,128)S(1)}, s32[2,6]{1,0:T(2,128)}, u32[]{:S(2)}) copy-start(s32[2,6]{1,0:T(2,128)} %param.6) | copy-start | bytes 148
  11.8 147.8 %all-to-all-start = ((f32[16,384,256]{1,2,0:T(8,128)}), f32[16,384,256]{1,2,0:T(8,128)}, u32[]{:S(2)}, u32[]{:S(2)}) async-start(f32[16,384,256]{1,2,0:T(8,128)} %stack.2), calls=%async_computation | async-start | bytes 12582912 | tf_op jit(solution)/shard_map/all_to_all | solution.py:19
  22.2 372.9 %reduce-scatter.2.cloned.1.call-start = ((), (), s32[]{:S(2)}) async-start(), calls=%async_computation.2 | async-start | bytes 2162688 | tf_op jit(solution)/shard_map/reduce_scatter | solution.py:24
Sparse Core Ops, SparseCore 0:
  170.4 224.5 reduce-scatter.1
